TPU v7x, 32 devices: a whole 2x2x4 slice. The times are simulated.
32 devices in a mesh: groups: 2 (over y), feat: 4 (over z), dp: 4 (over x, core).
Axes of the slice: x: 2, y: 2, z: 4, core: 2. Of those that a mesh axis runs over, the one named last changes fastest.
Arguments:
- features: bfloat16 [2048, 8192], P(('groups', 'dp'), 'feat'), parts along dimension 0, may hold values from -6 to 6
- bn_gain: float32 [8192], P('feat'), may hold values from 0.1 to 1.9
- bn_shift: float32 [8192], P('feat'), may hold values from -0.5 to 0.5
- weight: bfloat16 [8192, 8192], P('feat'), may hold values from -2 to 2
Outputs:
- covariance: float32 [16384, 8192], P(('groups', 'dp'), 'feat'), parts along dimension 0
- grad_in: bfloat16 [2048, 8192], P(('groups', 'dp'), 'feat'), parts along dimension 0
There are 2 independent parts, one for each index of `groups`. A program takes and returns all parts, laid end to end along the dimension named above; an argument that names none is the same for every part. Nothing has to cross between parts.
All inputs are finite; a program needn't handle non-finite values.
Results may differ from a plain program's by a relative error of at most 0.014.
Values may be sent and summed in bfloat16 or wider, within the bound.
A program may use at most 256 MiB of HBM per device.

v0:
```python
import jax
import jax.numpy as jnp
from jax import lax
from jax.sharding import PartitionSpec as P


def shards(features, bn_gain, bn_shift, weight):
    dp_count = lax.axis_size("dp")
    feat_count = lax.axis_size("feat")
    local_rows = features.shape[0]
    images = local_rows * dp_count
    hidden = features.astype(jnp.float32)
    col_sums, col_squares = lax.psum((jnp.sum(hidden, 0), jnp.sum(hidden * hidden, 0)), "dp")
    mean_h = col_sums / images
    var_h = col_squares / images - mean_h * mean_h
    normed = (hidden - mean_h) * lax.rsqrt(var_h + 1e-05) * bn_gain + bn_shift
    activated = jnp.maximum(normed, 0.0).astype(jnp.bfloat16)
    partial_value = jnp.dot(activated, weight, preferred_element_type=jnp.float32).astype(
        jnp.bfloat16
    )
    proj_f = lax.psum_scatter(partial_value, "feat", scatter_dimension=1, tiled=True).astype(
        jnp.float32
    )
    proj_mean = lax.psum(jnp.sum(proj_f, 0), "dp") / images
    centered = (proj_f - proj_mean).astype(jnp.bfloat16)
    cent_full = lax.all_gather(centered, "feat", axis=1, tiled=True)
    piece = lax.all_gather(centered, "dp", axis=0, tiled=True)
    cent_x = lax.all_to_all(cent_full, "dp", split_axis=1, concat_axis=0, tiled=True)
    gram = lax.psum(
        lax.dot_general(
            centered, piece, (((1,), (1,)), ((), ())), preferred_element_type=jnp.float32
        ),
        "feat",
    )
    piece_f = piece.astype(jnp.float32)
    proj_var = jnp.sum(piece_f * piece_f, 0) / (images - 1)
    spread = jnp.sqrt(proj_var + 0.0001)
    scale_up = images / (images - 1)
    active = jnp.where(spread < 1.0, 1.0 / spread, 0.0)
    factor = lax.all_gather(
        4.0 * scale_up * proj_var + 25.0 * scale_up * active, "feat", axis=0, tiled=True
    )
    scaled = (cent_full.astype(jnp.float32) * factor).astype(jnp.bfloat16)
    dims = (((1,), (1,)), ((), ()))
    through = lax.dot_general(cent_full, weight, dims, preferred_element_type=jnp.float32)
    direct = lax.dot_general(scaled, weight, dims, preferred_element_type=jnp.float32)
    through_all = lax.all_gather(through.astype(jnp.bfloat16), "dp", axis=0, tiled=True)
    covariance = lax.dot_general(
        cent_x, piece, (((0,), (0,)), ((), ())), preferred_element_type=jnp.float32
    ) / (images - 1)
    own = lax.axis_index("dp") * local_rows + jnp.arange(local_rows, dtype=jnp.int32)[:, None]
    same = own == jnp.arange(images, dtype=jnp.int32)[None, :]
    gram = gram * (4.0 * scale_up / (images - 1))
    diag = jnp.sum(jnp.where(same, gram, 0.0), 1, keepdims=True)
    rest = jnp.where(same, 0.0, gram).astype(jnp.bfloat16)
    grad_in = (
        jnp.dot(rest, through_all, preferred_element_type=jnp.float32) + diag * through - direct
    )
    return (covariance, grad_in.astype(jnp.bfloat16))


def solution(mesh):
    in_specs = (P(("groups", "dp"), "feat"), P("feat"), P("feat"), P("feat", None))
    out_specs = (P(("groups", "dp"), "feat"), P(("groups", "dp"), "feat"))
    return jax.shard_map(shards, mesh=mesh, in_specs=in_specs, out_specs=out_specs, check_vma=False)
```

profile of v0, /device:TPU:0, one launch (start us, length us, event | category | flops | bytes accessed | tf_op | source)
XLA Modules:
  0.0 372.7 jit_solution(6901499173663036275)
XLA Ops:
  7.2 0.0 reduce-scatter.2.cloned.1.call-start
  7.2 1.5 convert_reduce_fusion
  8.7 12.7 %all-reduce = (f32[2048]{0:T(1024)S(1)}, f32[2048]{0:T(1024)S(1)}) all-reduce(f32[2048]{0:T(1024)S(1)} %get-tuple-element.3, f32[2048]{0:T(1024)S(1)} %get-tuple-element.2), channel_id=1, replica_groups=mesh['groups'=2,'feat'=4,'dp'=4] {'dp'}, use_global_device_ids=true, to_apply=%region_3.0 | all-reduce | flops 4096 | bytes 32768 | tf_op jit(solution)/shard_map/psum | solution.py:13
  21.4 16.7 %convolution_convert_fusion = bf16[256,8192]{1,0:T(8,128)(2,1)} fusion(bf16[2048,8192]{1,0:T(8,128)(2,1)} %param.7, bf16[256,2048]{1,0:T(8,128)(2,1)} %param.4, f32[2048]{0:T(1024)} %param.6, f32[2048]{0:T(1024)} %param.5, f32[2048]{0:T(1024)S(1)} %get-tuple-element.7, f32[2048]{0:T(1024)S(1)} %get-tuple-element.6), kind=kOutput, calls=%fused_computation | convolution fusion | flops 8595701760 | bytes 38830080 | tf_op jit(solution)/shard_map/dot_general | solution.py:18
  38.1 0.0 reduce-scatter.2.cloned.1.call-update
  38.2 0.0 all-gather.6.cloned.1.call-start
  38.2 77.2 %reduce-scatter.2.cloned.1.call-done = bf16[256,2048]{1,0:T(8,128)(2,1)} async-done(((bf16[256,8192]{1,0:T(8,128)(2,1)}), bf16[256,2048]{1,0:T(8,128)(2,1)}) %reduce-scatter.2.cloned.1.call-update) | async-done | bytes 1048592 | tf_op jit(solution)/shard_map/reduce_scatter | solution.py:21
  115.4 1.4 convert_reduce_fusion.1
  116.8 7.0 %psum.30 = f32[2048]{0:T(1024)S(1)} all-reduce(f32[2048]{0:T(1024)S(1)} %convert_reduce_fusion.1), channel_id=1, replica_groups=mesh['groups'=2,'feat'=4,'dp'=4] {'dp'}, use_global_device_ids=true, to_apply=%region_6.0 | all-reduce | flops 2048 | bytes 16384 | tf_op jit(solution)/shard_map/psum | solution.py:24
  123.8 2.4 fusion.4
  126.3 0.0 all-gather.6.cloned.1.call-update
  126.3 0.0 all-gather.4.cloned.1.call-start
  126.3 0.7 all-gather.4.cloned.1.call-update
  127.0 0.0 all-reduce.3.cloned.1.call-start
  127.1 33.4 %all-gather.6.cloned.1.call-done = bf16[1024,2048]{1,0:T(8,128)(2,1)} async-done(((bf16[256,2048]{1,0:T(8,128)(2,1)}), bf16[1024,2048]{1,0:T(8,128)(2,1)}) %all-gather.6.cloned.1.call-update) | async-done | bytes 4194320 | tf_op jit(solution)/shard_map/all_gather | solution.py:27
  160.5 4.8 %fusion.24 = f32[256,1024]{1,0:T(8,128)} fusion(bf16[256,2048]{1,0:T(8,128)(2,1)} %fusion.4, bf16[1024,2048]{1,0:T(8,128)(2,1)} %all-gather.6.cloned.1.call-done), kind=kOutput, calls=%fused_computation.43 | convolution fusion | flops 1073741824 | bytes 6291456 | tf_op jit(solution)/shard_map/dot_general | solution.py:30
  165.3 0.0 all-reduce.3.cloned.1.call-update
  165.3 0.0 all-gather.8.cloned.1.call-start
  165.4 78.1 %all-gather.4.cloned.1.call-done = bf16[256,8192]{1,0:T(8,128)(2,1)} async-done(((bf16[256,2048]{1,0:T(8,128)(2,1)}), bf16[256,8192]{1,0:T(8,128)(2,1)}) %all-gather.4.cloned.1.call-update) | async-done | bytes 4194320 | tf_op jit(solution)/shard_map/all_gather | solution.py:26
  243.5 16.7 %fusion.23 = (bf16[256,2048]{1,0:T(8,128)(2,1)}, f32[256,2048]{1,0:T(8,128)S(1)}) fusion(bf16[256,8192]{1,0:T(8,128)(2,1)} %all-gather.4.cloned.1.call-done, bf16[2048,8192]{1,0:T(8,128)(2,1)} %param.7), kind=kOutput, calls=%fused_computation.42 | convolution fusion | flops 8590458880 | bytes 40894464 | tf_op jit(solution)/shard_map/dot_general | solution.py:45
  260.2 0.0 all-gather.8.cloned.1.call-update
  260.3 4.8 %copy.10 = bf16[32,4,8,2048]{3,2,0,1:T(8,128)(2,1)} copy(bf16[32,4,8,2048]{3,2,1,0:T(8,128)(2,1)} %bitcast.17) | data formatting | bytes 8388608 | tf_op jit(solution)/shard_map/all_to_all | solution.py:28
  265.1 4.9 %all-to-all-start = ((bf16[256,4,2048]{2,0,1:T(8,128)(2,1)}), bf16[256,4,2048]{2,0,1:T(8,128)(2,1)}, u32[]{:S(2)}, u32[]{:S(2)}) async-start(bf16[256,4,2048]{2,0,1:T(8,128)(2,1)} %bitcast.16), calls=%async_computation.1 | async-start | bytes 8388608 | tf_op jit(solution)/shard_map/all_to_all | solution.py:28
  270.0 3.1 multiply_reduce_fusion
  273.1 13.5 %all_gather.15 = f32[8192]{0:T(1024)S(1)} all-gather(f32[2048]{0:T(1024)S(1)} %multiply_add_fusion), channel_id=1, replica_groups=mesh['groups'=2,'feat'=4,'dp'=4] {'feat'}, dimensions={0}, use_global_device_ids=true | all-gather | bytes 40960 | tf_op jit(solution)/shard_map/all_gather | solution.py:40
  286.6 9.9 %all-reduce.3.cloned.1.call-done = f32[256,1024]{1,0:T(8,128)} async-done(((f32[256,1024]{1,0:T(8,128)}), f32[256,1024]{1,0:T(8,128)}) %all-reduce.3.cloned.1.call-update) | async-done | bytes 1048592 | tf_op jit(solution)/shard_map/psum | solution.py:29
  296.5 1.5 select_reduce_fusion
  298.0 30.3 %all-to-all-done = bf16[256,4,2048]{2,0,1:T(8,128)(2,1)} async-done(((bf16[256,4,2048]{2,0,1:T(8,128)(2,1)}), bf16[256,4,2048]{2,0,1:T(8,128)(2,1)}, u32[]{:S(2)}, u32[]{:S(2)}) %all-to-all-start) | async-done | bytes 4194336 | tf_op jit(solution)/shard_map/all_to_all | solution.py:28
  328.3 15.5 %convolution_multiply_fusion = f32[2048,2048]{1,0:T(8,128)} fusion(bf16[1024,2048]{1,0:T(8,128)(2,1)} %bitcast.1, bf16[1024,2048]{1,0:T(8,128)(2,1)} %all-gather.6.cloned.1.call-done), kind=kOutput, calls=%fused_computation.1 | convolution fusion | flops 8594128896 | bytes 25165824 | tf_op jit(solution)/shard_map/dot_general | solution.py:48
  343.9 0.0 copy-done
  343.9 4.9 %convolution_add_fusion = f32[256,2048]{1,0:T(8,128)} fusion(bf16[1024,2048]{1,0:T(8,128)(2,1)} %all-gather.8.cloned.1.call-done, f32[256,2048]{1,0:T(8,128)S(1)} %get-tuple-element.9, f32[256]{0:T(256)S(1)} %select_reduce_fusion, f32[256,1024]{1,0:T(8,128)S(1)} %copy-done, s32[256]{0:T(256)S(1)} %iota_add_fusion), kind=kOutput, calls=%fused_computation.12 | convolution fusion | flops 1075838976 | bytes 9439232 | tf_op jit(solution)/shard_map/dot_general | solution.py:57
  348.8 17.4 %fusion.3 = bf16[256,2048]{1,0:T(8,128)(2,1)} fusion(f32[256,2048]{1,0:T(8,128)} %convolution_add_fusion, bf16[2048,8192]{1,0:T(8,128)(2,1)} %param.7, bf16[256,8192]{1,0:T(8,128)(2,1)} %all-gather.4.cloned.1.call-done, f32[8192]{0:T(1024)S(1)} %all_gather.15), kind=kOutput, calls=%fused_computation.14 | convolution fusion | flops 8597274624 | bytes 40927232 | tf_op jit(solution)/shard_map/dot_general | solution.py:46
  (6 shorter events, 0.0 us)
Async XLA Ops:
  7.2 108.3 %reduce-scatter.2.cloned.1.call-start = ((), (), s32[]{:S(2)}) async-start(), calls=%async_computation.2 | async-start | bytes 5242880 | tf_op jit(solution)/shard_map/reduce_scatter | solution.py:21
  38.2 122.3 %all-gather.6.cloned.1.call-start = ((), (), s32[]{:S(2)}) async-start(), calls=%async_computation.4 | async-start | bytes 5242880 | tf_op jit(solution)/shard_map/all_gather | solution.py:27
  126.3 117.2 %all-gather.4.cloned.1.call-start = ((), (), s32[]{:S(2)}) async-start(), calls=%async_computation.3 | async-start | bytes 5242880 | tf_op jit(solution)/shard_map/all_gather | solution.py:26
  127.0 169.5 %all-reduce.3.cloned.1.call-start = ((), (), s32[]{:S(2)}) async-start(), calls=%async_computation.5 | async-start | bytes 2097152 | tf_op jit(solution)/shard_map/psum | solution.py:29
  165.3 178.5 %all-gather.8.cloned.1.call-start = ((), (), s32[]{:S(2)}) async-start(), calls=%async_computation.6 | async-start | bytes 5242880 | tf_op jit(solution)/shard_map/all_gather | solution.py:47
  265.1 63.3 %all-to-all-start = ((bf16[256,4,2048]{2,0,1:T(8,128)(2,1)}), bf16[256,4,2048]{2,0,1:T(8,128)(2,1)}, u32[]{:S(2)}, u32[]{:S(2)}) async-start(bf16[256,4,2048]{2,0,1:T(8,128)(2,1)} %bitcast.16), calls=%async_computation.1 | async-start | bytes 8388608 | tf_op jit(solution)/shard_map/all_to_all | solution.py:28
  328.3 15.5 %copy-start = (f32[256,1024]{1,0:T(8,128)S(1)}, f32[256,1024]{1,0:T(8,128)}, u32[]{:S(2)}) copy-start(f32[256,1024]{1,0:T(8,128)} %all-reduce.3.cloned.1.call-done) | copy-start | bytes 3145732
Sparse Core Ops, SparseCore 0:
  38.3 77.0 reduce-scatter.1
  126.4 34.0 all-gather.5
  162.7 80.7 all-gather.3
  245.9 50.6 all-reduce.2
  298.5 43.7 all-gather.7
where the time goes:
time: 373 us
  waiting for transfers between devices  230 us (62%)
  matrix products  76.1 us (20%)
  blocking collectives  33.1 us (9%)
  between operations  13.8 us (4%)
  other arithmetic  9.99 us (3%)
  starting transfers between devices  5.14 us (1%)
  local copies, waits for them, and re-layouts  4.82 us (1%)
    all_gather x1, waiting for transfers between devices, shards(): cent_full = lax.all_gather(centered, 'feat', axis=1, tiled=True)  78.1 us
    reduce_scatter x1, waiting for transfers between devices, shards(): lax.psum_scatter(partial_value, 'feat', scatter_dimension=1, tiled=True)  77.2 us
    all_gather x1, waiting for transfers between devices, shards(): piece = lax.all_gather(centered, 'dp', axis=0, tiled=True)  33.4 us
    all_to_all x1, waiting for transfers between devices, shards(): lax.all_to_all(cent_full, 'dp', split_axis=1, concat_axis=0, tiled=True)  30.3 us
    dot_general x1, matrix products, shards(): lax.dot_general(scaled, weight, dims, preferred_element_type=jnp.float32)  17.4 us
    dot_general x1, matrix products, shards(): lax.dot_general(cent_full, weight, dims, preferred_element_type=jnp.float32)  16.7 us
    dot_general x1, matrix products, shards(): jnp.dot(activated, weight, preferred_element_type=jnp.float32)  16.7 us
    dot_general x1, matrix products, shards(): lax.dot_general(cent_x, piece, (((0,), (0,)), ((), ())), preferred_elemen...  15.5 us
  transfers between devices with their start and end apart: 6, of which 5 were waited for; matrix products, arithmetic and copies ran while one was open for 12% of the time, Pallas kernels for 0%

commit v1 on v0

--- a/solution.py
+++ b/solution.py
@@ -2,6 +2,11 @@
 import jax.numpy as jnp
 from jax import lax
 from jax.sharding import PartitionSpec as P
+
+
+def _time_bands(in_array):
+    block_next = jnp.sum(lax.all_gather(in_array, "feat"), 0)
+    return block_next
 
 
 def shards(features, bn_gain, bn_shift, weight):
@@ -26,11 +31,10 @@
     cent_full = lax.all_gather(centered, "feat", axis=1, tiled=True)
     piece = lax.all_gather(centered, "dp", axis=0, tiled=True)
     cent_x = lax.all_to_all(cent_full, "dp", split_axis=1, concat_axis=0, tiled=True)
-    gram = lax.psum(
+    gram = _time_bands(
         lax.dot_general(
             centered, piece, (((1,), (1,)), ((), ())), preferred_element_type=jnp.float32
-        ),
-        "feat",
+        )
     )
     piece_f = piece.astype(jnp.float32)
     proj_var = jnp.sum(piece_f * piece_f, 0) / (images - 1)

time: 373 us -> 389 us (1.043)
  waiting for transfers between devices: 230 us -> 243 us
    all_gather x1, waiting for transfers between devices: 0.01 us -> 22.1 us  [shards(): lax.all_gather(through.astype(jnp.bfloat16), 'dp', axis=0, tiled=True)]
    psum x1 -> x0, waiting for transfers between devices: 9.88 us -> none  [shards(): lax.psum(lax.dot_general(centered, piece, (((1,), (1,)), ((), ())), prefe...]
  transfers between devices with their start and end apart: 6 -> 6, of which waited for: 5 -> 5; matrix products, arithmetic and copies ran while one was open for 12% -> 13% of each run, Pallas kernels for 0% -> 0%
where the time goes in v1:
time: 389 us
  waiting for transfers between devices  243 us (62%)
  matrix products  77.2 us (20%)
  blocking collectives  33.1 us (9%)
  between operations  13.8 us (4%)
  other arithmetic  11.5 us (3%)
  starting transfers between devices  5.07 us (1%)
  local copies, waits for them, and re-layouts  4.79 us (1%)
    all_gather x1, waiting for transfers between devices, shards(): cent_full = lax.all_gather(centered, 'feat', axis=1, tiled=True)  78.2 us
    reduce_scatter x1, waiting for transfers between devices, shards(): lax.psum_scatter(partial_value, 'feat', scatter_dimension=1, tiled=True)  77.2 us
    all_gather x1, waiting for transfers between devices, shards(): piece = lax.all_gather(centered, 'dp', axis=0, tiled=True)  33.4 us
    all_to_all x1, waiting for transfers between devices, shards(): lax.all_to_all(cent_full, 'dp', split_axis=1, concat_axis=0, tiled=True)  31.6 us
    all_gather x1, waiting for transfers between devices, shards(): lax.all_gather(through.astype(jnp.bfloat16), 'dp', axis=0, tiled=True)  22.1 us
    dot_general x1, matrix products, shards(): lax.dot_general(scaled, weight, dims, preferred_element_type=jnp.float32)  17.4 us
    dot_general x1, matrix products, shards(): lax.dot_general(cent_full, weight, dims, preferred_element_type=jnp.float32)  17.3 us
    dot_general x1, matrix products, shards(): jnp.dot(activated, weight, preferred_element_type=jnp.float32)  16.7 us
  transfers between devices with their start and end apart: 6, of which 5 were waited for; matrix products, arithmetic and copies ran while one was open for 13% of the time, Pallas kernels for 0%

profile of v1, /device:TPU:0, one launch (start us, length us, event | category | flops | bytes accessed | tf_op | source)
XLA Modules:
  0.0 388.8 jit_solution(5192971002771917382)
XLA Ops:
  7.2 0.0 reduce-scatter.2.cloned.1.call-start
  7.2 1.5 convert_reduce_fusion
  8.7 12.7 %all-reduce = (f32[2048]{0:T(1024)S(1)}, f32[2048]{0:T(1024)S(1)}) all-reduce(f32[2048]{0:T(1024)S(1)} %get-tuple-element.3, f32[2048]{0:T(1024)S(1)} %get-tuple-element.2), channel_id=1, replica_groups=mesh['groups'=2,'feat'=4,'dp'=4] {'dp'}, use_global_device_ids=true, to_apply=%region_3.0 | all-reduce | flops 4096 | bytes 32768 | tf_op jit(solution)/shard_map/psum | solution.py:18
  21.4 16.7 %convolution_convert_fusion = bf16[256,8192]{1,0:T(8,128)(2,1)} fusion(bf16[2048,8192]{1,0:T(8,128)(2,1)} %param.7, bf16[256,2048]{1,0:T(8,128)(2,1)} %param.4, f32[2048]{0:T(1024)} %param.6, f32[2048]{0:T(1024)} %param.5, f32[2048]{0:T(1024)S(1)} %get-tuple-element.7, f32[2048]{0:T(1024)S(1)} %get-tuple-element.6), kind=kOutput, calls=%fused_computation | convolution fusion | flops 8595701760 | bytes 38830080 | tf_op jit(solution)/shard_map/dot_general | solution.py:23
  38.1 0.0 reduce-scatter.2.cloned.1.call-update
  38.2 0.0 all-gather.8.cloned.1.call-start
  38.2 77.2 %reduce-scatter.2.cloned.1.call-done = bf16[256,2048]{1,0:T(8,128)(2,1)} async-done(((bf16[256,8192]{1,0:T(8,128)(2,1)}), bf16[256,2048]{1,0:T(8,128)(2,1)}) %reduce-scatter.2.cloned.1.call-update) | async-done | bytes 1048592 | tf_op jit(solution)/shard_map/reduce_scatter | solution.py:26
  115.4 1.4 convert_reduce_fusion.1
  116.8 7.0 %psum.23 = f32[2048]{0:T(1024)S(1)} all-reduce(f32[2048]{0:T(1024)S(1)} %convert_reduce_fusion.1), channel_id=1, replica_groups=mesh['groups'=2,'feat'=4,'dp'=4] {'dp'}, use_global_device_ids=true, to_apply=%region_6.0 | all-reduce | flops 2048 | bytes 16384 | tf_op jit(solution)/shard_map/psum | solution.py:29
  123.8 2.4 fusion.4
  126.3 0.0 all-gather.8.cloned.1.call-update
  126.3 0.0 all-gather.6.cloned.1.call-start
  126.3 0.7 all-gather.6.cloned.1.call-update
  127.0 0.0 all-gather.12.cloned.1.call-start
  127.1 33.4 %all-gather.8.cloned.1.call-done = bf16[1024,2048]{1,0:T(8,128)(2,1)} async-done(((bf16[256,2048]{1,0:T(8,128)(2,1)}), bf16[1024,2048]{1,0:T(8,128)(2,1)}) %all-gather.8.cloned.1.call-update) | async-done | bytes 4194320 | tf_op jit(solution)/shard_map/all_gather | solution.py:32
  160.5 4.8 %fusion.24 = f32[256,1024]{1,0:T(8,128)} fusion(bf16[256,2048]{1,0:T(8,128)(2,1)} %fusion.4, bf16[1024,2048]{1,0:T(8,128)(2,1)} %all-gather.8.cloned.1.call-done), kind=kOutput, calls=%fused_computation.43 | convolution fusion | flops 1073741824 | bytes 6291456 | tf_op jit(solution)/shard_map/dot_general | solution.py:35
  165.3 0.0 all-gather.12.cloned.1.call-update
  165.3 0.0 all-gather.10.cloned.1.call-start
  165.3 78.2 %all-gather.6.cloned.1.call-done = bf16[256,8192]{1,0:T(8,128)(2,1)} async-done(((bf16[256,2048]{1,0:T(8,128)(2,1)}), bf16[256,8192]{1,0:T(8,128)(2,1)}) %all-gather.6.cloned.1.call-update) | async-done | bytes 4194320 | tf_op jit(solution)/shard_map/all_gather | solution.py:31
  243.5 17.3 %fusion.23 = (bf16[256,2048]{1,0:T(8,128)(2,1)}, f32[256,2048]{1,0:T(8,128)S(1)}) fusion(bf16[256,8192]{1,0:T(8,128)(2,1)} %all-gather.6.cloned.1.call-done, bf16[2048,8192]{1,0:T(8,128)(2,1)} %param.7), kind=kOutput, calls=%fused_computation.42 | convolution fusion | flops 8590458880 | bytes 40894464 | tf_op jit(solution)/shard_map/dot_general | solution.py:49
  260.9 0.0 all-gather.10.cloned.1.call-update
  260.9 4.8 %copy.11 = bf16[32,4,8,2048]{3,2,0,1:T(8,128)(2,1)} copy(bf16[32,4,8,2048]{3,2,1,0:T(8,128)(2,1)} %bitcast.18) | data formatting | bytes 8388608 | tf_op jit(solution)/shard_map/all_to_all | solution.py:33
  265.7 4.9 %all-to-all-start = ((bf16[256,4,2048]{2,0,1:T(8,128)(2,1)}), bf16[256,4,2048]{2,0,1:T(8,128)(2,1)}, u32[]{:S(2)}, u32[]{:S(2)}) async-start(bf16[256,4,2048]{2,0,1:T(8,128)(2,1)} %bitcast.17), calls=%async_computation.1 | async-start | bytes 8388608 | tf_op jit(solution)/shard_map/all_to_all | solution.py:33
  270.6 3.1 multiply_reduce_fusion
  273.7 13.5 %all_gather.23 = f32[8192]{0:T(1024)S(1)} all-gather(f32[2048]{0:T(1024)S(1)} %multiply_add_fusion), channel_id=1, replica_groups=mesh['groups'=2,'feat'=4,'dp'=4] {'feat'}, dimensions={0}, use_global_device_ids=true | all-gather | bytes 40960 | tf_op jit(solution)/shard_map/all_gather | solution.py:44
  287.2 31.6 %all-to-all-done = bf16[256,4,2048]{2,0,1:T(8,128)(2,1)} async-done(((bf16[256,4,2048]{2,0,1:T(8,128)(2,1)}), bf16[256,4,2048]{2,0,1:T(8,128)(2,1)}, u32[]{:S(2)}, u32[]{:S(2)}) %all-to-all-start) | async-done | bytes 4194336 | tf_op jit(solution)/shard_map/all_to_all | solution.py:33
  318.8 16.0 %convolution_multiply_fusion = f32[2048,2048]{1,0:T(8,128)} fusion(bf16[1024,2048]{1,0:T(8,128)(2,1)} %bitcast.1, bf16[1024,2048]{1,0:T(8,128)(2,1)} %all-gather.8.cloned.1.call-done), kind=kOutput, calls=%fused_computation.1 | convolution fusion | flops 8594128896 | bytes 25165824 | tf_op jit(solution)/shard_map/dot_general | solution.py:52
  334.8 2.8 reduce_sum.57
  337.6 0.3 select_reduce_fusion
  337.9 22.1 %all-gather.10.cloned.1.call-done = bf16[1024,2048]{1,0:T(8,128)(2,1)} async-done(((bf16[256,2048]{1,0:T(8,128)(2,1)}), bf16[1024,2048]{1,0:T(8,128)(2,1)}) %all-gather.10.cloned.1.call-update) | async-done | bytes 4194320 | tf_op jit(solution)/shard_map/all_gather | solution.py:51
  359.9 4.9 %convolution_add_fusion = f32[256,2048]{1,0:T(8,128)} fusion(bf16[1024,2048]{1,0:T(8,128)(2,1)} %all-gather.10.cloned.1.call-done, f32[256,2048]{1,0:T(8,128)S(1)} %get-tuple-element.9, f32[256]{0:T(256)S(1)} %select_reduce_fusion, f32[256,1024]{1,0:T(8,128)S(1)} %reduce_sum.57, s32[256]{0:T(256)S(1)} %iota_add_fusion), kind=kOutput, calls=%fused_computation.12 | convolution fusion | flops 1075838976 | bytes 9439232 | tf_op jit(solution)/shard_map/dot_general | solution.py:61
  364.9 17.4 %fusion.3 = bf16[256,2048]{1,0:T(8,128)(2,1)} fusion(f32[256,2048]{1,0:T(8,128)} %convolution_add_fusion, bf16[2048,8192]{1,0:T(8,128)(2,1)} %param.7, bf16[256,8192]{1,0:T(8,128)(2,1)} %all-gather.6.cloned.1.call-done, f32[8192]{0:T(1024)S(1)} %all_gather.23), kind=kOutput, calls=%fused_computation.14 | convolution fusion | flops 8597274624 | bytes 40927232 | tf_op jit(solution)/shard_map/dot_general | solution.py:50
  (5 shorter events, 0.0 us)
Async XLA Ops:
  7.2 108.3 %reduce-scatter.2.cloned.1.call-start = ((), (), s32[]{:S(2)}) async-start(), calls=%async_computation.2 | async-start | bytes 5242880 | tf_op jit(solution)/shard_map/reduce_scatter | solution.py:26
  38.2 122.3 %all-gather.8.cloned.1.call-start = ((), (), s32[]{:S(2)}) async-start(), calls=%async_computation.4 | async-start | bytes 5242880 | tf_op jit(solution)/shard_map/all_gather | solution.py:32
  126.3 117.2 %all-gather.6.cloned.1.call-start = ((), (), s32[]{:S(2)}) async-start(), calls=%async_computation.3 | async-start | bytes 5242880 | tf_op jit(solution)/shard_map/all_gather | solution.py:31
  127.0 207.8 %all-gather.12.cloned.1.call-start = ((), (), s32[]{:S(2)}) async-start(), calls=%async_computation.6 | async-start | bytes 5242880 | tf_op jit(solution)/shard_map/all_gather | solution.py:8
  165.3 194.6 %all-gather.10.cloned.1.call-start = ((), (), s32[]{:S(2)}) async-start(), calls=%async_computation.5 | async-start | bytes 5242880 | tf_op jit(solution)/shard_map/all_gather | solution.py:51
  265.7 53.1 %all-to-all-start = ((bf16[256,4,2048]{2,0,1:T(8,128)(2,1)}), bf16[256,4,2048]{2,0,1:T(8,128)(2,1)}, u32[]{:S(2)}, u32[]{:S(2)}) async-start(bf16[256,4,2048]{2,0,1:T(8,128)(2,1)} %bitcast.17), calls=%async_computation.1 | async-start | bytes 8388608 | tf_op jit(solution)/shard_map/all_to_all | solution.py:33
Sparse Core Ops, SparseCore 0:
  38.3 77.0 reduce-scatter.1
  126.4 34.0 all-gather.7
  162.7 80.7 all-gather.5
  245.0 79.7 all-gather.11
  326.8 33.0 all-gather.9
